TPU v7x, 32 devices: a whole 2x2x4 slice. The times are simulated.
32 devices in a mesh: dp: 2 (over y), expert: 16 (over z, x, core).
Axes of the slice: x: 2, y: 2, z: 4, core: 2. Of those that a mesh axis runs over, the one named last changes fastest.
Arguments:
- tokens: bfloat16 [256, 4096], P(('dp', 'expert')), may hold values from -6 to 6
- expert_ids: int32 [256, 8], P(('dp', 'expert')), may hold values from 0 to 15, all different within a row; in each aligned block of 8 rows (0 to 7, 8 to 15, ...) at most 6 rows name the same one
- gate_values: float32 [256, 8], P(('dp', 'expert')), may hold values from 0.05 to 1
- w_gate: bfloat16 [16, 4096, 2048], P('expert', None, 'dp'), may hold values from -0.09375 to 0.09375
- w_up: bfloat16 [16, 4096, 2048], P('expert', None, 'dp'), may hold values from -0.09375 to 0.09375
- w_down: bfloat16 [16, 2048, 4096], P('expert', 'dp'), may hold values from -0.125 to 0.125
- s_gate: bfloat16 [4096, 2048], P(None, 'dp'), may hold values from -0.09375 to 0.09375
- s_up: bfloat16 [4096, 2048], P(None, 'dp'), may hold values from -0.09375 to 0.09375
- s_down: bfloat16 [2048, 4096], P('dp'), may hold values from -0.125 to 0.125
Outputs:
- mixed: bfloat16 [256, 4096], P(('dp', 'expert'))
Inputs may be any that keep to these rules, and one draw needn't show every extreme that they name: `expert_ids`: each row names 8 different experts; the 8 rows of one device name one expert at most 6 times.
All inputs are finite; a program needn't handle non-finite values.
Results may differ from a plain program's by a relative error of at most 0.0054.
Values may be sent and summed in bfloat16 or wider, within the bound.
A program may use at most 128 MiB of HBM per device.

v0:
```python
import jax
import jax.numpy as jnp
from jax import lax
from jax.sharding import PartitionSpec as P


def swiglu(rows, gate_w, up_w, down_w):
    gate = jnp.dot(rows, gate_w, preferred_element_type=jnp.float32)
    up = jnp.dot(rows, up_w, preferred_element_type=jnp.float32)
    hidden = (jax.nn.silu(gate) * up).astype(jnp.bfloat16)
    return jnp.dot(hidden, down_w, preferred_element_type=jnp.float32)


def slot_tables(route_ids, route_gates, experts, capacity):
    row_count, picks = route_ids.shape
    listed = route_ids.reshape(-1)
    expert_range = jnp.arange(experts, dtype=jnp.int32)
    marks = (listed[:, None] == expert_range[None, :]).astype(jnp.int32)
    earlier = jnp.cumsum(marks, axis=0) - marks
    position = jnp.sum(earlier * marks, axis=1)
    slot_index = (listed * capacity + position).reshape(row_count, picks)
    slot_range = jnp.arange(experts * capacity, dtype=jnp.int32)
    matches = slot_index[:, :, None] == slot_range[None, None, :]
    picker = jnp.any(matches, axis=1).astype(jnp.bfloat16)
    combiner = jnp.sum(jnp.where(matches, route_gates[:, :, None], jnp.float32(0.0)), axis=1)
    return (picker, combiner)


def dispatch_rows(picker, source_rows):
    placed = jnp.einsum("rs,rd->sd", picker, source_rows, preferred_element_type=jnp.float32)
    return placed.astype(jnp.bfloat16)


def per_device(tokens, expert_ids, gate_values, w_gate, w_up, w_down, s_gate, s_up, s_down):
    experts = lax.axis_size("expert")
    groups = lax.axis_size("dp")
    own_rows, width = tokens.shape
    picks = expert_ids.shape[1]
    capacity = max(2, min(own_rows, 3 * own_rows * picks // (2 * experts)))
    gate_local = w_gate[0]
    up_local = w_up[0]
    down_local = w_down[0]
    column = lax.all_gather(tokens, "dp", axis=0, tiled=True)
    column_ids, column_gates = (
        lax.all_gather(expert_ids, "dp", axis=0, tiled=True),
        lax.all_gather(gate_values, "dp", axis=0, tiled=True),
    )
    column_cap = capacity * groups
    picker, combiner = slot_tables(column_ids, column_gates, experts, column_cap)
    outgoing = dispatch_rows(picker, column).reshape(experts, column_cap, width)
    arrived = lax.all_to_all(outgoing, "expert", split_axis=0, concat_axis=0, tiled=True)
    items = arrived.shape[1]
    partial_value = swiglu(
        arrived.reshape(experts * items, width), gate_local, up_local, down_local
    )
    partial_value = partial_value.astype(jnp.bfloat16).reshape(experts, items, width)
    returned = lax.all_to_all(partial_value, "expert", split_axis=0, concat_axis=0, tiled=True)
    returned_rows = returned.reshape(experts * column_cap, width)
    routed = jnp.dot(
        combiner,
        returned_rows.astype(jnp.float32),
        precision=lax.Precision.HIGHEST,
        preferred_element_type=jnp.float32,
    )
    mixed = lax.psum_scatter(
        swiglu(column, s_gate, s_up, s_down) + routed, "dp", scatter_dimension=0, tiled=True
    )
    return mixed.astype(jnp.bfloat16)


def solution(mesh):
    placed = (
        P(("dp", "expert"), None),
        P(("dp", "expert"), None),
        P(("dp", "expert"), None),
        P("expert", None, "dp"),
        P("expert", None, "dp"),
        P("expert", "dp", None),
        P(None, "dp"),
        P(None, "dp"),
        P("dp", None),
    )
    return jax.shard_map(
        per_device, mesh=mesh, in_specs=placed, out_specs=P(("dp", "expert"), None), check_vma=False
    )
```

profile of v0, /device:TPU:0, one launch (start us, length us, event | category | flops | bytes accessed | tf_op | source)
XLA Modules:
  0.0 174.3 jit_solution(16177684296198305586)
XLA Ops:
  6.5 5.4 %all_gather.10 = s32[16,8]{1,0:T(8,128)S(1)} all-gather(s32[8,8]{1,0:T(8,128)} %param.10), channel_id=1, replica_groups=mesh['dp'=2,'expert'=16] {'dp'}, dimensions={0}, use_global_device_ids=true | all-gather | bytes 768 | tf_op jit(solution)/shard_map/all_gather | solution.py:45
  12.0 0.1 eq.28
  12.1 0.1 fusion.21
  12.2 0.2 reduce_window_sum.11
  12.3 0.2 select_reduce_fusion.1
  12.5 0.1 reduce_sum.21
  12.6 0.1 fusion.20
  12.8 5.2 %all_gather.9 = bf16[16,4096]{1,0:T(8,128)(2,1)S(1)} all-gather(bf16[8,4096]{1,0:T(8,128)(2,1)} %param.9), channel_id=1, replica_groups=mesh['dp'=2,'expert'=16] {'dp'}, dimensions={0}, use_global_device_ids=true | all-gather | bytes 196608 | tf_op jit(solution)/shard_map/all_gather | solution.py:43
  17.9 1.8 %convolution_convert_fusion = bf16[192,4096]{1,0:T(8,128)(2,1)} fusion(pred[16,192]{1,0:T(8,128)(4,1)S(1)} %fusion.20, bf16[16,4096]{1,0:T(8,128)(2,1)S(1)} %all_gather.9), kind=kOutput, calls=%fused_computation.7 | convolution fusion | flops 25952256 | bytes 1707008 | tf_op jit(solution)/shard_map/rs,rd->sd/dot_general | solution.py:30
  19.7 2.3 %reshape.21 = bf16[16,12,4096]{2,1,0:T(8,128)(2,1)S(1)} reshape(bf16[192,4096]{1,0:T(8,128)(2,1)} %convolution_convert_fusion) | data formatting | bytes 3145728 | tf_op jit(solution)/shard_map/reshape | solution.py:50
  22.0 53.6 %all_to_all.10 = bf16[16,12,4096]{2,1,0:T(8,128)(2,1)} all-to-all(bf16[16,12,4096]{2,1,0:T(8,128)(2,1)S(1)} %reshape.21), channel_id=1, replica_groups=mesh['dp'=2,'expert'=16] {'expert'}, dimensions={0} | all-to-all | bytes 3145728 | tf_op jit(solution)/shard_map/all_to_all | solution.py:51
  75.6 2.5 %reshape.22 = bf16[192,4096]{1,0:T(8,128)(2,1)S(1)} reshape(bf16[16,12,4096]{2,1,0:T(8,128)(2,1)} %all_to_all.10) | data formatting | bytes 3145728 | tf_op jit(solution)/shard_map/reshape | solution.py:54
  78.1 5.2 %fusion.4 = f32[192,1024]{1,0:T(8,128)S(1)} fusion(bf16[192,4096]{1,0:T(8,128)(2,1)S(1)} %reshape.22, bf16[1,4096,1024]{2,1,0:T(8,128)(2,1)} %param.12), kind=kOutput, calls=%fused_computation.4 | convolution fusion | flops 1610612736 | bytes 10747904 | tf_op jit(solution)/shard_map/dot_general | solution.py:8
  83.2 0.0 copy-start
  83.2 10.5 %fusion.6 = bf16[192,4096]{1,0:T(8,128)(2,1)} fusion(bf16[1,1024,4096]{2,1,0:T(8,128)(2,1)} %param.14, bf16[192,4096]{1,0:T(8,128)(2,1)S(1)} %reshape.22, bf16[1,4096,1024]{2,1,0:T(8,128)(2,1)} %param.13, f32[192,1024]{1,0:T(8,128)S(1)} %fusion.4), kind=kOutput, calls=%fused_computation.6 | convolution fusion | flops 3223191552 | bytes 20709376 | tf_op jit(solution)/shard_map/dot_general | solution.py:11
  93.7 3.4 %reshape.23 = bf16[16,12,4096]{2,1,0:T(8,128)(2,1)} reshape(bf16[192,4096]{1,0:T(8,128)(2,1)} %fusion.6) | data formatting | bytes 3145728 | tf_op jit(solution)/shard_map/reshape | solution.py:56
  97.1 5.1 %all-to-all-start.1 = ((bf16[16,12,4096]{2,1,0:T(8,128)(2,1)}), bf16[16,12,4096]{2,1,0:T(8,128)(2,1)S(1)}, u32[]{:S(2)}, u32[]{:S(2)}) async-start(bf16[16,12,4096]{2,1,0:T(8,128)(2,1)} %reshape.23), calls=%async_computation.1 | async-start | bytes 4194304 | tf_op jit(solution)/shard_map/all_to_all | solution.py:57
  102.2 0.0 reduce-scatter.2.cloned.1.call-start
  102.3 0.0 copy-done
  102.3 4.3 %all_gather.11 = f32[16,8]{1,0:T(8,128)S(1)} all-gather(f32[8,8]{1,0:T(8,128)S(1)} %copy-done), channel_id=1, replica_groups=mesh['dp'=2,'expert'=16] {'dp'}, dimensions={0}, use_global_device_ids=true | all-gather | bytes 768 | tf_op jit(solution)/shard_map/all_gather | solution.py:46
  106.6 0.1 select_reduce_fusion
  106.8 4.6 %fusion.30 = f32[16,1024]{1,0:T(8,128)S(1)} fusion(bf16[16,4096]{1,0:T(8,128)(2,1)S(1)} %all_gather.9, bf16[4096,1024]{1,0:T(8,128)(2,1)} %param.15), kind=kOutput, calls=%fused_computation.30 | convolution fusion | flops 134217728 | bytes 8585216 | tf_op jit(solution)/shard_map/dot_general | solution.py:8
  111.3 8.1 %fusion.16 = f32[16,4096]{1,0:T(8,128)S(1)} fusion(bf16[1024,4096]{1,0:T(8,128)(2,1)} %param.17, bf16[16,4096]{1,0:T(8,128)(2,1)S(1)} %all_gather.9, bf16[4096,1024]{1,0:T(8,128)(2,1)} %param.16, f32[16,1024]{1,0:T(8,128)S(1)} %fusion.30), kind=kOutput, calls=%fused_computation.13 | convolution fusion | flops 268533760 | bytes 17235968 | tf_op jit(solution)/shard_map/dot_general | solution.py:11
  119.4 23.9 %all-to-all-done.1 = bf16[16,12,4096]{2,1,0:T(8,128)(2,1)S(1)} async-done(((bf16[16,12,4096]{2,1,0:T(8,128)(2,1)}), bf16[16,12,4096]{2,1,0:T(8,128)(2,1)S(1)}, u32[]{:S(2)}, u32[]{:S(2)}) %all-to-all-start.1) | async-done | bytes 1572896 | tf_op jit(solution)/shard_map/all_to_all | solution.py:57
  143.4 1.3 reshape.24
  144.7 2.8 %convolution_add_fusion = f32[16,4096]{1,0:T(8,128)} fusion(f32[16,4096]{1,0:T(8,128)S(1)} %fusion.16, f32[16,192]{1,0:T(8,128)S(1)} %select_reduce_fusion, bf16[192,4096]{1,0:T(8,128)(2,1)} %reshape.24), kind=kOutput, calls=%fused_computation.8 | convolution fusion | flops 151060480 | bytes 2109440 | tf_op jit(solution)/shard_map/dot_general | solution.py:59
  147.5 0.0 reduce-scatter.2.cloned.1.call-update
  147.5 18.4 %reduce-scatter.2.cloned.1.call-done = f32[8,4096]{1,0:T(8,128)} async-done(((f32[16,4096]{1,0:T(8,128)}), f32[8,4096]{1,0:T(8,128)}) %reduce-scatter.2.cloned.1.call-update) | async-done | bytes 131088 | tf_op jit(solution)/shard_map/reduce_scatter | solution.py:65
  165.9 1.5 convert_element_type.25
  (1 shorter events, 0.0 us)
Async XLA Ops:
  83.2 19.1 %copy-start = (f32[8,8]{1,0:T(8,128)S(1)}, f32[8,8]{1,0:T(8,128)}, u32[]{:S(2)}) copy-start(f32[8,8]{1,0:T(8,128)} %param.11) | copy-start | bytes 772
  97.1 46.2 %all-to-all-start.1 = ((bf16[16,12,4096]{2,1,0:T(8,128)(2,1)}), bf16[16,12,4096]{2,1,0:T(8,128)(2,1)S(1)}, u32[]{:S(2)}, u32[]{:S(2)}) async-start(bf16[16,12,4096]{2,1,0:T(8,128)(2,1)} %reshape.23), calls=%async_computation.1 | async-start | bytes 4194304 | tf_op jit(solution)/shard_map/all_to_all | solution.py:57
  102.2 63.7 %reduce-scatter.2.cloned.1.call-start = ((), (), s32[]{:S(2)}) async-start(), calls=%async_computation.3 | async-start | bytes 393216 | tf_op jit(solution)/shard_map/reduce_scatter | solution.py:65
Sparse Core Ops, SparseCore 0:
  147.7 18.1 reduce-scatter.1
where the time goes:
time: 175 us; the launch traced here: 174 us
  blocking collectives  68.5 us (39%)
  waiting for transfers between devices  42.3 us (24%)
  matrix products  32.9 us (19%)
  between operations  13.5 us (8%)
  local copies, waits for them, and re-layouts  9.69 us (6%)
  starting transfers between devices  5.15 us (3%)
  other arithmetic  2.24 us (1%)
    all_to_all x1, blocking collectives, per_device(): lax.all_to_all(outgoing, 'expert', split_axis=0, concat_axis=0, tiled=True)  53.6 us
    all_to_all x1, waiting for transfers between devices, per_device(): lax.all_to_all(partial_value, 'expert', split_axis=0, concat_axis=0, tile...  23.9 us
    dot_general x2, matrix products, swiglu(): return jnp.dot(hidden, down_w, preferred_element_type=jnp.float32)  18.5 us
    reduce_scatter x1, waiting for transfers between devices, per_device(): lax.psum_scatter(swiglu(column, s_gate, s_up, s_down) + routed, 'dp', sca...  18.4 us
    dot_general x2, matrix products, swiglu(): gate = jnp.dot(rows, gate_w, preferred_element_type=jnp.float32)  9.75 us
    all_gather x1, blocking collectives, per_device(): lax.all_gather(expert_ids, 'dp', axis=0, tiled=True)  5.45 us
    all_gather x1, blocking collectives, per_device(): column = lax.all_gather(tokens, 'dp', axis=0, tiled=True)  5.15 us
    all_to_all x1, starting transfers between devices, per_device(): lax.all_to_all(partial_value, 'expert', split_axis=0, concat_axis=0, tile...  5.11 us
  transfers between devices with their start and end apart: 2, of which 2 were waited for; matrix products, arithmetic and copies ran while one was open for 7% of the time, Pallas kernels for 0%

commit v1 on v0

--- a/solution.py
+++ b/solution.py
@@ -1,7 +1,15 @@
+import functools
+
 import jax
 import jax.numpy as jnp
 from jax import lax
+from jax.experimental import pallas as pl
+from jax.experimental.pallas import tpu as pltpu
 from jax.sharding import PartitionSpec as P
+
+LANES = 128
+BF16 = jnp.bfloat16
+F32 = jnp.float32
 
 
 def swiglu(rows, gate_w, up_w, down_w):
@@ -16,7 +24,9 @@
     listed = route_ids.reshape(-1)
     expert_range = jnp.arange(experts, dtype=jnp.int32)
     marks = (listed[:, None] == expert_range[None, :]).astype(jnp.int32)
-    earlier = jnp.cumsum(marks, axis=0) - marks
+    step = jnp.arange(listed.shape[0], dtype=jnp.int32)
+    before = (step[None, :] < step[:, None]).astype(jnp.bfloat16)
+    earlier = jnp.dot(before, marks.astype(jnp.bfloat16), preferred_element_type=jnp.float32).astype(jnp.int32)
     position = jnp.sum(earlier * marks, axis=1)
     slot_index = (listed * capacity + position).reshape(row_count, picks)
     slot_range = jnp.arange(experts * capacity, dtype=jnp.int32)
@@ -31,7 +41,7 @@
     return placed.astype(jnp.bfloat16)
 
 
-def per_device(tokens, expert_ids, gate_values, w_gate, w_up, w_down, s_gate, s_up, s_down):
+def exchange_layer(tokens, expert_ids, gate_values, w_gate, w_up, w_down, s_gate, s_up, s_down):
     experts = lax.axis_size("expert")
     groups = lax.axis_size("dp")
     own_rows, width = tokens.shape
@@ -68,6 +78,331 @@
     return mixed.astype(jnp.bfloat16)
 
 
+HERE, Y_NEXT, X_NEXT, ACROSS = 3, 2, 1, 0
+DOWN_PARTS = 4
+TILE = 256
+
+
+def fused_kernel(depth_z, token_ref, ids_ref, gates_ref, wg_hbm, wu_hbm, wd_hbm, sg_hbm, su_hbm, sd_hbm, out_ref,
+                 blocks, rows, wg, wu, wd, sgu, sd, hidden, shared, coef_ref, kept, core_out, core_in, flat_out, flat_in,
+                 side_out, side_in, line_out, line_in, load_sem, gsend, grecv, csend, crecv, asend, arecv, bsend, brecv,
+                 lsend, lrecv):
+    own, width = token_ref.shape
+    experts = lax.axis_size("expert")
+    place = lax.axis_index("expert")
+    group = lax.axis_index("dp")
+    core = lax.rem(place, 2)
+    across_x = lax.rem(lax.div(place, 2), 2)
+    other_core = {"dp": group, "expert": place + 1 - 2 * core}
+    x_next = {"dp": group, "expert": place + 2 - 4 * across_x}
+    y_next = {"dp": 1 - group, "expert": place}
+
+    def along_z(steps):
+        return {"dp": group, "expert": lax.rem(place + 4 * steps, experts)}
+
+    loads = []
+
+    def load(src, dst):
+        copy = pltpu.make_async_copy(src, dst, load_sem.at[len(loads)])
+        copy.start()
+        loads.append(copy)
+
+    piece = sd.shape[0]
+    sharers = experts * piece // sg_hbm.shape[1]
+    first = pl.multiple_of(lax.div(place, sharers) * piece, piece)
+    load(sg_hbm.at[:, pl.ds(first, piece)], sgu.at[:, pl.ds(0, piece)])
+    load(su_hbm.at[:, pl.ds(first, piece)], sgu.at[:, pl.ds(piece, piece)])
+    inner = wg.shape[1]
+    for at in range(0, inner, TILE):
+        load(wg_hbm.at[0, :, pl.ds(at, TILE)], wg.at[:, pl.ds(at, TILE)])
+        load(wu_hbm.at[0, :, pl.ds(at, TILE)], wu.at[:, pl.ds(at, TILE)])
+    load(sd_hbm.at[pl.ds(first, piece), :], sd)
+    part = width // DOWN_PARTS
+    for n in range(DOWN_PARTS):
+        load(wd_hbm.at[0, :, pl.ds(n * part, part)], wd.at[:, pl.ds(n * part, part)])
+
+    def slot(own_core, column, turn):
+        return (own_core * 4 + column) * depth_z + turn
+
+    mine = slot(1, HERE, 0)
+    blocks[mine, :, pl.ds(0, width)] = token_ref[...]
+    lane = lax.broadcasted_iota(jnp.int32, (own, LANES), 1)
+    expert_of = lax.rem(lane, experts)
+    term_of = lax.div(lane, experts)
+    gate = jnp.zeros((own, LANES), F32)
+    for k in range(ids_ref.shape[1]):
+        gate = gate + jnp.where(ids_ref[:, k:k + 1] == expert_of, gates_ref[:, k:k + 1], 0.0)
+    high = gate.astype(BF16).astype(F32)
+    middle = (gate - high).astype(BF16).astype(F32)
+    low = gate - high - middle
+    terms = jnp.where(term_of == 0, high, jnp.where(term_of == 1, middle, jnp.where(term_of == 2, low, 0.0)))
+    blocks[mine, :, pl.ds(width, LANES)] = terms.astype(BF16)
+
+    barrier = pltpu.get_barrier_semaphore()
+    peers = [other_core, x_next, y_next] + [along_z(k) for k in range(1, depth_z)]
+    for peer in peers:
+        pl.semaphore_signal(barrier, inc=1, device_id=peer, device_id_type=pl.DeviceIdType.MESH)
+    pl.semaphore_wait(barrier, len(peers))
+
+    started = []
+
+    def push(src, dst, send, recv, peer):
+        copy = pltpu.make_async_remote_copy(src_ref=src, dst_ref=dst, send_sem=send, recv_sem=recv, device_id=peer,
+                                            device_id_type=pl.DeviceIdType.MESH)
+        copy.start()
+        started.append(copy)
+
+    gathers = [0]
+
+    def pass_on(here, there, peer):
+        push(blocks.at[here], blocks.at[there], gsend.at[gathers[0]], grecv.at[there], peer)
+        gathers[0] += 1
+
+    def arrived(at):
+        pltpu.make_async_copy(blocks.at[at], blocks.at[at], grecv.at[at]).wait()
+
+    def to_core(column, turn):
+        pass_on(slot(1, column, turn), slot(0, column, turn), other_core)
+
+    def to_x(column, turn):
+        pass_on(slot(1, column, turn), slot(1, column ^ 2, turn), x_next)
+
+    def to_y(column, turn):
+        pass_on(slot(1, column, turn), slot(1, column ^ 1, turn), y_next)
+
+    half = depth_z // 2
+    order = [0]
+    for k in range(1, half + 1):
+        order += [k] if 2 * k == depth_z else [k, depth_z - k]
+
+    def spread(turn):
+        if turn:
+            arrived(slot(1, HERE, turn))
+        to_x(HERE, turn)
+        to_y(HERE, turn)
+        if turn == 0:
+            for k in order[1:]:
+                pass_on(mine, slot(1, HERE, depth_z - k), along_z(k))
+        to_core(HERE, turn)
+
+    def relay(turn):
+        arrived(slot(1, X_NEXT, turn))
+        if turn < half:
+            to_y(X_NEXT, turn)
+        to_core(X_NEXT, turn)
+        arrived(slot(1, Y_NEXT, turn))
+        if turn >= half:
+            to_x(Y_NEXT, turn)
+        to_core(Y_NEXT, turn)
+
+    spread(order[0])
+    for before, turn in zip(order, order[1:]):
+        spread(turn)
+        relay(before)
+    relay(order[-1])
+    for turn in order:
+        arrived(slot(1, ACROSS, turn))
+        to_core(ACROSS, turn)
+    for turn in order:
+        for column in (HERE, X_NEXT, Y_NEXT, ACROSS):
+            arrived(slot(0, column, turn))
+
+    def pack(i, carry):
+        pair = [blocks[2 * i + j, :, pl.ds(0, width)].astype(F32) for j in range(2)]
+        tail = [blocks[2 * i + j, :, pl.ds(width, LANES)].astype(F32) for j in range(2)]
+        at = pl.ds(pl.multiple_of(i * 2 * own, 2 * own), 2 * own)
+        rows[at, :] = jnp.concatenate(pair, axis=0).astype(BF16)
+        lanes = lax.broadcasted_iota(jnp.int32, (2 * own, LANES), 1)
+        ours = (lax.rem(lanes, experts) == place) & (lanes < 3 * experts)
+        coef_ref[at, :] = jnp.sum(jnp.where(ours, jnp.concatenate(tail, axis=0), 0.0), axis=1, keepdims=True)
+        return carry
+
+    total = rows.shape[0]
+    lax.fori_loop(0, total // (2 * own), pack, 0)
+
+    for copy in loads[:2]:
+        copy.wait()
+    both = jnp.dot(rows[...], sgu[...], preferred_element_type=F32)
+    value = jax.nn.silu(both[:, :piece]) * both[:, piece:]
+    share_of = lax.div(lax.broadcasted_iota(jnp.int32, (total, piece), 1), piece // sharers)
+    shared[...] = jnp.where(share_of == lax.rem(place, sharers), value, 0.0).astype(BF16)
+
+    for i in range(inner // TILE):
+        loads[2 + 2 * i].wait()
+        loads[3 + 2 * i].wait()
+
+    def hidden_tile(j, carry):
+        at = pl.ds(pl.multiple_of(j * TILE, TILE), TILE)
+        gated = jnp.dot(rows[...], wg[:, at], preferred_element_type=F32)
+        up = jnp.dot(rows[...], wu[:, at], preferred_element_type=F32)
+        hidden[:, at] = (jax.nn.silu(gated) * up).astype(BF16)
+        return carry
+
+    lax.fori_loop(0, inner // TILE, hidden_tile, 0)
+    for copy in loads[2 + 2 * (inner // TILE):]:
+        copy.wait()
+
+    split = total // 2
+    column_rows = depth_z * own
+    cut = half * own
+
+    def down(n):
+        def tile(j, carry):
+            src = pl.ds(pl.multiple_of(n * part + j * TILE, TILE), TILE)
+            dst = pl.ds(pl.multiple_of(j * TILE, TILE), TILE)
+            routed = jnp.dot(hidden[...], wd[:, src], preferred_element_type=F32)
+            common = jnp.dot(shared[...], sd[:, src], preferred_element_type=F32)
+            value = routed * coef_ref[...] + common
+            core_out[n, :, dst] = value[:split].astype(BF16)
+            kept[n, :, dst] = value[split:]
+            return carry
+
+        lax.fori_loop(0, part // TILE, tile, 0)
+        push(core_out.at[n], core_in.at[n], csend.at[n], crecv.at[n], other_core)
+
+    def landed(ref, sem):
+        pltpu.make_async_copy(ref, ref, sem).wait()
+
+    def flat(n):
+        landed(core_in.at[n], crecv.at[n])
+        at = pl.ds(0, column_rows)
+        flat_out[n, :, :] = (kept[n, at, :] + core_in[n, at, :].astype(F32)).astype(BF16)
+        push(flat_out.at[n, pl.ds(0, cut)], flat_in.at[n, pl.ds(0, cut)], asend.at[2 * n], arecv.at[2 * n], y_next)
+        push(flat_out.at[n, pl.ds(cut, column_rows - cut)], flat_in.at[n, pl.ds(cut, column_rows - cut)],
+             asend.at[2 * n + 1], arecv.at[2 * n + 1], x_next)
+
+    def side(n):
+        at = pl.ds(column_rows, 2 * column_rows)
+        summed = kept[n, at, :] + core_in[n, at, :].astype(F32)
+        landed(flat_in.at[n, pl.ds(0, cut)], arecv.at[2 * n])
+        landed(flat_in.at[n, pl.ds(cut, column_rows - cut)], arecv.at[2 * n + 1])
+        came = flat_in[n].astype(F32)
+        side_out[n, 0] = jnp.concatenate([summed[:cut] + came[:cut], summed[cut:column_rows]], axis=0).astype(BF16)
+        side_out[n, 1] = jnp.concatenate(
+            [summed[column_rows:column_rows + cut], summed[column_rows + cut:] + came[cut:]], axis=0).astype(BF16)
+        push(side_out.at[n, 0], side_in.at[n, 0], bsend.at[2 * n], brecv.at[2 * n], x_next)
+        push(side_out.at[n, 1], side_in.at[n, 1], bsend.at[2 * n + 1], brecv.at[2 * n + 1], y_next)
+
+    def line(n):
+        at = pl.ds(3 * column_rows, column_rows)
+        summed = kept[n, at, :] + core_in[n, at, :].astype(F32)
+        landed(side_in.at[n, 0], brecv.at[2 * n])
+        landed(side_in.at[n, 1], brecv.at[2 * n + 1])
+        summed = summed + side_in[n, 0].astype(F32) + side_in[n, 1].astype(F32)
+        kept[n, pl.ds(0, own), :] = summed[:own]
+        for k in order[1:]:
+            line_out[n, k] = summed[k * own:(k + 1) * own].astype(BF16)
+            push(line_out.at[n, k], line_in.at[n, depth_z - k], lsend.at[n * depth_z + k],
+                 lrecv.at[n * depth_z + depth_z - k], along_z(k))
+
+    def finish(n):
+        result = kept[n, pl.ds(0, own), :]
+        for k in order[1:]:
+            landed(line_in.at[n, k], lrecv.at[n * depth_z + k])
+            result = result + line_in[n, k].astype(F32)
+        out_ref[:, pl.ds(n * part, part)] = result.astype(out_ref.dtype)
+
+    stages = (down, flat, side, line, finish)
+    for step in range(DOWN_PARTS + len(stages) - 1):
+        for lag, stage in enumerate(stages):
+            if 0 <= step - lag < DOWN_PARTS:
+                stage(step - lag)
+    for copy in started:
+        copy.wait_send()
+
+
+def fused_bytes(tokens, w_gate, devices):
+    own, width = tokens.shape
+    inner = w_gate.shape[2]
+    total = own * devices
+    weights = 2 * (3 * width * inner + 3 * width * LANES)
+    gathered = 2 * total * (3 * (width + LANES))
+    return weights + gathered + 10 * total * width + 4 * total * LANES
+
+
+def fused_layer(tokens, expert_ids, gate_values, w_gate, w_up, w_down, s_gate, s_up, s_down):
+    experts = lax.axis_size("expert")
+    devices = experts * lax.axis_size("dp")
+    depth_z = experts // 4
+    own, width = tokens.shape
+    inner = w_gate.shape[2]
+    total = own * devices
+    part = width // DOWN_PARTS
+    split = total // 2
+    column_rows = depth_z * own
+    sends = 16 // 4 * depth_z + 3 * depth_z * 4
+    dma = pltpu.SemaphoreType.DMA
+    scratch = [
+        pltpu.VMEM((devices, own, width + LANES), BF16),
+        pltpu.VMEM((total, width), BF16),
+        pltpu.VMEM((width, inner), BF16),
+        pltpu.VMEM((width, inner), BF16),
+        pltpu.VMEM((inner, width), BF16),
+        pltpu.VMEM((width, 2 * LANES), BF16),
+        pltpu.VMEM((LANES, width), BF16),
+        pltpu.VMEM((total, inner), BF16),
+        pltpu.VMEM((total, LANES), BF16),
+        pltpu.VMEM((total, 1), F32),
+        pltpu.VMEM((DOWN_PARTS, split, part), F32),
+        pltpu.VMEM((DOWN_PARTS, split, part), BF16),
+        pltpu.VMEM((DOWN_PARTS, split, part), BF16),
+        pltpu.VMEM((DOWN_PARTS, column_rows, part), BF16),
+        pltpu.VMEM((DOWN_PARTS, column_rows, part), BF16),
+        pltpu.VMEM((DOWN_PARTS, 2, column_rows, part), BF16),
+        pltpu.VMEM((DOWN_PARTS, 2, column_rows, part), BF16),
+        pltpu.VMEM((DOWN_PARTS, depth_z, own, part), BF16),
+        pltpu.VMEM((DOWN_PARTS, depth_z, own, part), BF16),
+        dma((3 + 2 * (inner // TILE) + DOWN_PARTS,)),
+        dma((sends,)),
+        dma((devices,)),
+        dma((DOWN_PARTS,)),
+        dma((DOWN_PARTS,)),
+        dma((2 * DOWN_PARTS,)),
+        dma((2 * DOWN_PARTS,)),
+        dma((2 * DOWN_PARTS,)),
+        dma((2 * DOWN_PARTS,)),
+        dma((depth_z * DOWN_PARTS,)),
+        dma((depth_z * DOWN_PARTS,)),
+    ]
+    vmem = pl.BlockSpec(memory_space=pltpu.VMEM)
+    hbm = pl.BlockSpec(memory_space=pl.ANY)
+    return pl.pallas_call(
+        functools.partial(fused_kernel, depth_z),
+        out_shape=jax.ShapeDtypeStruct((own, width), BF16),
+        in_specs=[vmem] * 3 + [hbm] * 6,
+        out_specs=vmem,
+        scratch_shapes=scratch,
+        compiler_params=pltpu.CompilerParams(collective_id=0, has_side_effects=True,
+                                             vmem_limit_bytes=VMEM_BYTES),
+        cost_estimate=pl.CostEstimate(flops=6 * total * width * (inner + LANES),
+                                      bytes_accessed=6 * width * (inner + LANES), transcendentals=total * inner),
+    )(tokens, expert_ids, gate_values, w_gate, w_up, w_down, s_gate, s_up, s_down)
+
+
+VMEM_BYTES = 60 * 2**20
+
+
+def per_device(tokens, expert_ids, gate_values, w_gate, w_up, w_down, s_gate, s_up, s_down):
+    experts = lax.axis_size("expert")
+    groups = lax.axis_size("dp")
+    own, width = tokens.shape
+    args = (tokens, expert_ids, gate_values, w_gate, w_up, w_down, s_gate, s_up, s_down)
+    inner = w_gate.shape[2]
+    pieces = s_gate.shape[1] // LANES
+    fits = (
+        groups == 2
+        and experts % 8 == 0
+        and 3 * experts <= LANES
+        and own % 8 == 0
+        and width % (DOWN_PARTS * TILE) == 0
+        and inner % TILE == 0
+        and s_gate.shape[1] % LANES == 0
+        and experts % pieces == 0
+        and fused_bytes(tokens, w_gate, groups * experts) <= VMEM_BYTES
+    )
+    return fused_layer(*args) if fits else exchange_layer(*args)
+
+
 def solution(mesh):
     placed = (
         P(("dp", "expert"), None),

time: 175 us -> 55.7 us (0.32)
  blocking collectives: 68.5 us -> 0 us
  Pallas kernels: 0 us -> 54 us
  waiting for transfers between devices: 42.3 us -> 0 us
  matrix products: 32.9 us -> 0 us
  between operations: 13.5 us -> 0.01 us
  local copies, waits for them, and re-layouts: 9.69 us -> 1.47 us
  starting transfers between devices: 5.15 us -> 0 us
  other arithmetic: 2.24 us -> 0 us
    pallas_call x0 -> x1, Pallas kernels: none -> 54 us  [fused_layer(): pl.pallas_call(functools.partial(fused_kernel, depth_z), out_shape=jax.Sh...]
    all_to_all x1 -> x0, blocking collectives: 53.6 us -> none  [per_device(): lax.all_to_all(outgoing, 'expert', split_axis=0, concat_axis=0, tiled=True)]
    dot_general x6 -> x0, matrix products: 32.9 us -> none  [the longest x2 18.5 us: swiglu(): return jnp.dot(hidden, down_w, preferred_element_type=jnp.float32)]
    all_to_all x1 -> x0, waiting for transfers between devices: 23.9 us -> none  [per_device(): lax.all_to_all(partial_value, 'expert', split_axis=0, concat_axis=0, tile...]
    reduce_scatter x1 -> x0, waiting for transfers between devices: 18.4 us -> none  [per_device(): lax.psum_scatter(swiglu(column, s_gate, s_up, s_down) + routed, 'dp', sca...]
    all_gather x3 -> x0, blocking collectives: 14.9 us -> none  [the longest x1 5.45 us: per_device(): lax.all_gather(expert_ids, 'dp', axis=0, tiled=True)]
    reshape x4 -> x0, local copies, waits for them, and re-layouts: 9.52 us -> none  [the longest x1 3.41 us: per_device(): partial_value.astype(jnp.bfloat16).reshape(experts, items, width)]
    all_to_all x1 -> x0, starting transfers between devices: 5.11 us -> none  [per_device(): lax.all_to_all(partial_value, 'expert', split_axis=0, concat_axis=0, tile...]
  transfers between devices with their start and end apart: 2 -> 0, of which waited for: 2 -> 0; matrix products, arithmetic and copies ran while one was open for 7% -> 0% of each run, Pallas kernels for 0% -> 0%
where the time goes in v1:
time: 55.7 us; the launch traced here: 55.5 us
  Pallas kernels  54 us (97%)
  local copies, waits for them, and re-layouts  1.47 us (3%)
    pallas_call x1, Pallas kernels, fused_layer(): pl.pallas_call(functools.partial(fused_kernel, depth_z), out_shape=jax.Sh...  54 us
    unnamed x1, local copies, waits for them, and re-layouts  1.47 us

profile of v1, /device:TPU:0, one launch (start us, length us, event | category | flops | bytes accessed | tf_op | source)
XLA Modules:
  0.0 55.5 jit_solution(18122740699974345800)
XLA Ops:
  0.0 54.0 %shard_map.91 = bf16[8,4096]{1,0:T(8,128)(2,1)} custom-call(bf16[8,4096]{1,0:T(8,128)(2,1)} %token_ref.1, s32[8,8]{1,0:T(8,128)} %ids_ref.1, f32[8,8]{1,0:T(8,128)} %gates_ref.1, bf16[1,4096,1024]{2,1,0:T(8,128)(2,1)} %wg_hbm.1, bf16[1,4096,1024]{2,1,0:T(8,128)(2,1)} %wu_hbm.1, bf16[1,1024,4096]{2,1,0:T(8,128)(2,1)} %wd_hbm.1, bf16[4096,1024]{1,0:T(8,128)(2,1)} %sg_hbm.1, ...), custom_call_target="tpu_custom_call" | custom-call | flops 7247757312 | bytes 28311552 | tf_op jit(solution)/shard_map/pallas_call | solution.py:369
  54.0 1.5 %copy.11 = bf16[8,4096]{1,0:T(8,128)(2,1)} copy(bf16[8,4096]{1,0:T(8,128)(2,1)} %shard_map.91) | data formatting | bytes 131072
